TPU v7x, 32 devices: a whole 2x2x4 slice. The times are simulated.
32 devices in a mesh: dp: 8 (over z, y), tensor: 4 (over x, core).
Axes of the slice: x: 2, y: 2, z: 4, core: 2. Of those that a mesh axis runs over, the one named last changes fastest.
Arguments:
- tokens: bfloat16 [8192, 1024], P('dp')
- cotangent: bfloat16 [8192, 1024], P('dp'), may hold values from -6 to 6
- segments: int32 [8192], P('dp'), may hold values from 0 to 5, as said below
- positions: int32 [8192], P('dp'), may hold values from 0 to 5094, as said below
- attn_gain: bfloat16 [1024], P('dp'), may hold values from 0.099609375 to 1.8984375
- w_query: bfloat16 [1024, 1024], P('dp', 'tensor'), may hold values from -0.1875 to 0.1875
- w_key: bfloat16 [1024, 512], P('dp', 'tensor'), may hold values from -0.1875 to 0.1875
- w_value: bfloat16 [1024, 512], P('dp', 'tensor'), may hold values from -0.1875 to 0.1875
- query_gain: bfloat16 [64], P('dp'), may hold values from 0.5 to 2
- key_gain: bfloat16 [64], P('dp'), may hold values from 0.5 to 2
- w_out: bfloat16 [1024, 1024], P('tensor', 'dp'), may hold values from -1.5 to 1.5
- ffn_gain: bfloat16 [1024], P('dp'), may hold values from 0.099609375 to 1.8984375
- w_gate: bfloat16 [1024, 4608], P('dp', 'tensor'), may hold values from -0.1875 to 0.1875
- w_up: bfloat16 [1024, 4608], P('dp', 'tensor'), may hold values from -0.1875 to 0.1875
- w_down: bfloat16 [4608, 1024], P('tensor', 'dp'), may hold values from -0.1875 to 0.1875
Outputs:
- output: bfloat16 [8192, 1024], P(('dp', 'tensor'))
- tokens_grad: float32 [8192, 1024], P('dp')
- attn_gain_grad: float32 [1024], P('dp')
- query_grad: float32 [1024, 1024], P('dp', 'tensor')
- key_grad: float32 [1024, 512], P('dp', 'tensor')
- value_grad: float32 [1024, 512], P('dp', 'tensor')
- query_gain_grad: float32 [64], P('dp')
- key_gain_grad: float32 [64], P('dp')
- out_grad: float32 [1024, 1024], P('tensor', 'dp')
- ffn_gain_grad: float32 [1024], P('dp')
- gate_grad: float32 [1024, 4608], P('dp', 'tensor')
- up_grad: float32 [1024, 4608], P('dp', 'tensor')
- down_grad: float32 [4608, 1024], P('tensor', 'dp')
Inputs may be any that keep to these rules, and one draw needn't show every extreme that they name: `segments`: within each sequence of 1024 tokens the numbers start at 0 and never fall; every run but a sequence's last is a document of 200 to 1000 tokens, the last is at most 1000. Within a document the positions rise by one from token to token; a document's first position lies below 4096.
All inputs are finite; a program needn't handle non-finite values.
Results may differ from a plain program's by a relative error of at most 0.028.
Values may be sent and summed in bfloat16 or wider, within the bound.
A program may use at most 192 MiB of HBM per device.

v0:
```python
import jax
import jax.numpy as jnp
from jax import lax
from jax.sharding import PartitionSpec as P

HD = 64
LEN = 1024


EPSILON = 1e-05
ROPE_BASE = 1000000.0
MASKED = -1e30


def norm_rows(values, gain):
    return values * lax.rsqrt(jnp.mean(values * values, axis=-1, keepdims=True) + EPSILON) * gain


def rotate_half(values, cosine, sine_table):
    halfway = values.shape[-1] // 2
    first_half = values[..., :halfway]
    second_half = values[..., halfway:]
    return jnp.concatenate(
        [
            first_half * cosine - second_half * sine_table,
            second_half * cosine + first_half * sine_table,
        ],
        axis=-1,
    )


def rope_tables(positions):
    halfway = HD // 2
    frequency = ROPE_BASE ** (-(jnp.arange(halfway, dtype=jnp.float32) * 2.0 / HD))
    angle_grid = positions.astype(jnp.float32)[:, None] * frequency[None, :]
    return (jnp.cos(angle_grid)[:, None, :], jnp.sin(angle_grid)[:, None, :])


def matmul(left, right):
    return jnp.dot(left, right, preferred_element_type=jnp.float32)


def matmul_tn(left, right):
    return lax.dot_general(
        left, right, (((0,), (0,)), ((), ())), preferred_element_type=jnp.float32
    )


def matmul_nt(left, right):
    return lax.dot_general(
        left, right, (((1,), (1,)), ((), ())), preferred_element_type=jnp.float32
    )


def block_scores(query_block, key_rows, seq_segments, first_row, last_row):
    score_scale = query_block.shape[-1] ** (-0.5)
    places = jnp.arange(seq_segments.shape[0])
    scores = (
        jnp.einsum("tkgd,skd->kgts", query_block, key_rows, preferred_element_type=jnp.float32)
        * score_scale
    )
    allowed = (places[first_row:last_row, None] >= places[None, :last_row]) & (
        seq_segments[first_row:last_row, None] == seq_segments[None, :last_row]
    )
    return jnp.where(allowed, scores, MASKED)


def attend(operands):
    queries, keys_low, values_low, seq_segments = operands
    length = queries.shape[0]
    block_rows = min(512, length)
    pieces = []
    lse_parts = []
    for first_row in range(0, length, block_rows):
        last_row = first_row + block_rows
        scores = block_scores(
            queries[first_row:last_row], keys_low[:last_row], seq_segments, first_row, last_row
        )
        row_max = jnp.max(scores, axis=-1, keepdims=True)
        shifted = jnp.exp(scores - row_max)
        totals = jnp.sum(shifted, axis=-1, keepdims=True)
        probabilities = (shifted / totals).astype(jnp.bfloat16)
        pieces.append(
            jnp.einsum(
                "kgts,skd->tkgd",
                probabilities,
                values_low[:last_row],
                preferred_element_type=jnp.float32,
            )
        )
        lse_parts.append(row_max + jnp.log(totals))
    return (jnp.concatenate(pieces, axis=0), jnp.concatenate(lse_parts, axis=2))


def attend_back(operands):
    queries, keys_low, values_low, seq_segments, lse_rows, grad_mixed = operands
    length = queries.shape[0]
    block_rows = min(512, length)
    score_scale = queries.shape[-1] ** (-0.5)
    key_total = jnp.zeros(keys_low.shape, jnp.float32)
    value_total = jnp.zeros(values_low.shape, jnp.float32)
    query_pieces = []
    for first_row in range(0, length, block_rows):
        last_row = first_row + block_rows
        scores = block_scores(
            queries[first_row:last_row], keys_low[:last_row], seq_segments, first_row, last_row
        )
        probabilities = jnp.exp(scores - lse_rows[:, :, first_row:last_row])
        grad_block = grad_mixed[first_row:last_row]
        grad_probs = jnp.einsum(
            "tkgd,skd->kgts", grad_block, values_low[:last_row], preferred_element_type=jnp.float32
        )
        row_terms = jnp.sum(probabilities * grad_probs, axis=-1, keepdims=True)
        grad_scores = (probabilities * (grad_probs - row_terms)).astype(jnp.bfloat16)
        query_pieces.append(
            jnp.einsum(
                "kgts,skd->tkgd",
                grad_scores,
                keys_low[:last_row],
                preferred_element_type=jnp.float32,
            )
            * score_scale
        )
        padding = ((0, length - last_row), (0, 0), (0, 0))
        key_part = (
            jnp.einsum(
                "kgts,tkgd->skd",
                grad_scores,
                queries[first_row:last_row],
                preferred_element_type=jnp.float32,
            )
            * score_scale
        )
        value_part = jnp.einsum(
            "kgts,tkgd->skd",
            probabilities.astype(jnp.bfloat16),
            grad_block,
            preferred_element_type=jnp.float32,
        )
        key_total = key_total + jnp.pad(key_part, padding)
        value_total = value_total + jnp.pad(value_part, padding)
    return (jnp.concatenate(query_pieces, axis=0), key_total, value_total)


def swiglu(gate_in, up_in):
    return jax.nn.silu(gate_in) * up_in


def body(
    tokens,
    cotangent,
    segments,
    positions,
    attn_gain,
    w_query,
    w_key,
    w_value,
    query_gain,
    key_gain,
    w_out,
    ffn_gain,
    w_gate,
    w_up,
    w_down,
):
    attn_set = (
        lax.all_gather(attn_gain, "dp", axis=0, tiled=True),
        lax.all_gather(w_query, "dp", axis=0, tiled=True),
        lax.all_gather(w_key, "dp", axis=0, tiled=True),
        lax.all_gather(w_value, "dp", axis=0, tiled=True),
        lax.all_gather(query_gain, "dp", axis=0, tiled=True),
        lax.all_gather(key_gain, "dp", axis=0, tiled=True),
        lax.all_gather(w_out, "dp", axis=1, tiled=True),
    )
    gain_first, query_full, key_full, value_full, qgain_full, kgain_full, out_full = attn_set
    token_count = tokens.shape[0]
    seq_count = token_count // LEN
    local_heads = query_full.shape[1] // HD
    local_kv = key_full.shape[1] // HD
    group_size = local_heads // local_kv
    share_rows = token_count // lax.axis_size("tensor")
    own_start = lax.axis_index("tensor") * share_rows
    inputs = tokens.astype(jnp.float32)
    attn_scale = gain_first.astype(jnp.float32)
    normed_float, attn_norm_back = jax.vjp(norm_rows, inputs, attn_scale)
    normed = normed_float.astype(jnp.bfloat16)
    query_raw = matmul(normed, query_full).reshape(token_count, local_heads, HD)
    key_raw = matmul(normed, key_full).reshape(token_count, local_kv, HD)
    value_low = (
        matmul(normed, value_full).astype(jnp.bfloat16).reshape(seq_count, LEN, local_kv, HD)
    )
    cosine, sine_table = rope_tables(positions)

    def head_prep(raw_rows, gain_rows):
        return rotate_half(norm_rows(raw_rows, gain_rows), cosine, sine_table)

    query_prep, query_back = jax.vjp(head_prep, query_raw, qgain_full.astype(jnp.float32))
    key_prep, key_back = jax.vjp(head_prep, key_raw, kgain_full.astype(jnp.float32))
    query_low = query_prep.astype(jnp.bfloat16).reshape(seq_count, LEN, local_kv, group_size, HD)
    key_low = key_prep.astype(jnp.bfloat16).reshape(seq_count, LEN, local_kv, HD)
    seq_segments = segments.reshape(seq_count, LEN)
    mixed, lse_rows = lax.map(attend, (query_low, key_low, value_low, seq_segments))
    mixed_low = mixed.reshape(token_count, local_heads * HD).astype(jnp.bfloat16)
    attn_part = matmul(mixed_low, out_full)
    ffn_set = (
        lax.all_gather(ffn_gain, "dp", axis=0, tiled=True),
        lax.all_gather(w_gate, "dp", axis=0, tiled=True),
        lax.all_gather(w_up, "dp", axis=0, tiled=True),
        lax.all_gather(w_down, "dp", axis=1, tiled=True),
    )
    gain_second, gate_full, up_full, down_full = ffn_set
    ffn_scale = gain_second.astype(jnp.float32)
    residual = inputs + lax.psum(attn_part, "tensor")
    ffn_float, ffn_norm_back = jax.vjp(norm_rows, residual, ffn_scale)
    normed_ffn = ffn_float.astype(jnp.bfloat16)
    residual_rows = lax.dynamic_slice_in_dim(residual, own_start, share_rows, 0)
    gate_value = matmul(normed_ffn, gate_full)
    up_value = matmul(normed_ffn, up_full)
    hidden_float, swiglu_back = jax.vjp(swiglu, gate_value, up_value)
    hidden = hidden_float.astype(jnp.bfloat16)
    ffn_share = lax.psum_scatter(
        matmul(
            lax.slice_in_dim(hidden, 0, share_rows * lax.axis_size("tensor"), axis=0), down_full
        ).astype(jnp.bfloat16),
        "tensor",
        scatter_dimension=0,
        tiled=True,
    ).astype(jnp.float32)
    output = (residual_rows + ffn_share).astype(jnp.bfloat16)
    grad_output = cotangent.astype(jnp.float32)
    down_grad = matmul_tn(hidden, cotangent)
    grad_hidden = matmul_nt(cotangent, down_full)
    grad_gate, grad_up = swiglu_back(grad_hidden)
    gate_low = grad_gate.astype(jnp.bfloat16)
    up_low = grad_up.astype(jnp.bfloat16)
    gate_grad = matmul_tn(normed_ffn, gate_low)
    up_grad = matmul_tn(normed_ffn, up_low)
    ffn_input_part = matmul_nt(gate_low, gate_full) + matmul_nt(up_low, up_full)
    residual_part, ffn_gain_part = ffn_norm_back(lax.psum(ffn_input_part, "tensor"))
    grad_residual = residual_part + grad_output
    grad_attn_low = grad_residual.astype(jnp.bfloat16)
    out_grad = matmul_tn(mixed_low, grad_attn_low)
    grad_mixed = (
        matmul_nt(grad_attn_low, out_full)
        .astype(jnp.bfloat16)
        .reshape(seq_count, LEN, local_kv, group_size, HD)
    )
    grad_query, grad_key, grad_value = lax.map(
        attend_back, (query_low, key_low, value_low, seq_segments, lse_rows, grad_mixed)
    )
    grad_qraw, grad_qgain = query_back(grad_query.reshape(token_count, local_heads, HD))
    grad_kraw, grad_kgain = key_back(grad_key.reshape(token_count, local_kv, HD))
    query_low_grad = grad_qraw.reshape(token_count, local_heads * HD).astype(jnp.bfloat16)
    key_low_grad = grad_kraw.reshape(token_count, local_kv * HD).astype(jnp.bfloat16)
    value_low_grad = grad_value.reshape(token_count, local_kv * HD).astype(jnp.bfloat16)
    query_weight_grad = matmul_tn(normed, query_low_grad)
    key_weight_grad = matmul_tn(normed, key_low_grad)
    value_weight_grad = matmul_tn(normed, value_low_grad)
    attn_input_part = (
        matmul_nt(query_low_grad, query_full)
        + matmul_nt(key_low_grad, key_full)
        + matmul_nt(value_low_grad, value_full)
    )
    attn_input_grad, qgain_total, kgain_total = lax.psum(
        (attn_input_part, grad_qgain, grad_kgain), "tensor"
    )
    input_part, attn_gain_grad = attn_norm_back(attn_input_grad)
    tokens_grad = input_part + grad_residual
    ffn_grads = (
        lax.psum_scatter(ffn_gain_part, "dp", scatter_dimension=0, tiled=True),
        lax.psum_scatter(gate_grad, "dp", scatter_dimension=0, tiled=True),
        lax.psum_scatter(up_grad, "dp", scatter_dimension=0, tiled=True),
        lax.psum_scatter(down_grad, "dp", scatter_dimension=1, tiled=True),
    )
    attn_grads = (
        lax.psum_scatter(attn_gain_grad, "dp", scatter_dimension=0, tiled=True),
        lax.psum_scatter(query_weight_grad, "dp", scatter_dimension=0, tiled=True),
        lax.psum_scatter(key_weight_grad, "dp", scatter_dimension=0, tiled=True),
        lax.psum_scatter(value_weight_grad, "dp", scatter_dimension=0, tiled=True),
        lax.psum_scatter(qgain_total, "dp", scatter_dimension=0, tiled=True),
        lax.psum_scatter(kgain_total, "dp", scatter_dimension=0, tiled=True),
        lax.psum_scatter(out_grad, "dp", scatter_dimension=1, tiled=True),
    )
    return (
        output,
        tokens_grad,
        attn_grads[0],
        attn_grads[1],
        attn_grads[2],
        attn_grads[3],
        attn_grads[4],
        attn_grads[5],
        attn_grads[6],
        ffn_grads[0],
        ffn_grads[1],
        ffn_grads[2],
        ffn_grads[3],
    )


def solution(mesh):
    placed = (
        P("dp", None),
        P("dp", None),
        P("dp"),
        P("dp"),
        P("dp"),
        P("dp", "tensor"),
        P("dp", "tensor"),
        P("dp", "tensor"),
        P("dp"),
        P("dp"),
        P("tensor", "dp"),
        P("dp"),
        P("dp", "tensor"),
        P("dp", "tensor"),
        P("tensor", "dp"),
    )
    return jax.shard_map(
        body,
        mesh=mesh,
        in_specs=placed,
        out_specs=(
            P(("dp", "tensor"), None),
            P("dp", None),
            P("dp"),
            P("dp", "tensor"),
            P("dp", "tensor"),
            P("dp", "tensor"),
            P("dp"),
            P("dp"),
            P("tensor", "dp"),
            P("dp"),
            P("dp", "tensor"),
            P("dp", "tensor"),
            P("tensor", "dp"),
        ),
        check_vma=False,
    )
```

profile of v0, /device:TPU:0, one launch (start us, length us, event | category | flops | bytes accessed | tf_op | source)
XLA Modules:
  0.0 1180.3 jit_solution(1932035219222922275)
XLA Ops:
  11.8 23.1 %all-reduce.14 = (bf16[64]{0:T(256)(128)(2,1)S(1)}, bf16[64]{0:T(256)(128)(2,1)S(1)}) all-reduce(bf16[64]{0:T(256)(128)(2,1)S(1)} %dynamic-update-slice.1, bf16[64]{0:T(256)(128)(2,1)S(1)} %dynamic-update-slice), channel_id=1, replica_groups=mesh['dp'=8,'tensor'=4] {'dp'}, use_global_device_ids=true, to_apply=%add.7 | all-reduce | flops 128 | bytes 512
  37.9 16.4 %all-gather = bf16[8,1,128]{2,1,0:T(2,128)(2,1)S(1)} all-gather(bf16[1,1,128]{2,1,0:T(2,128)(2,1)} %bitcast.204), channel_id=1, replica_groups=mesh['dp'=8,'tensor'=4] {'dp'}, dimensions={0}, use_global_device_ids=true | all-gather | bytes 2304 | tf_op jit(solution)/shard_map/all_gather | solution.py:167
  55.1 31.0 %all_gather.35 = bf16[1024,128]{1,0:T(8,128)(2,1)S(1)} all-gather(bf16[128,128]{1,0:T(8,128)(2,1)} %param.21), channel_id=1, replica_groups=mesh['dp'=8,'tensor'=4] {'dp'}, dimensions={0}, use_global_device_ids=true | all-gather | bytes 294912 | tf_op jit(solution)/shard_map/all_gather | solution.py:169
  86.1 31.1 %all_gather.34 = bf16[1024,128]{1,0:T(8,128)(2,1)S(1)} all-gather(bf16[128,128]{1,0:T(8,128)(2,1)} %param.22), channel_id=1, replica_groups=mesh['dp'=8,'tensor'=4] {'dp'}, dimensions={0}, use_global_device_ids=true | all-gather | bytes 294912 | tf_op jit(solution)/shard_map/all_gather | solution.py:170
  117.2 31.7 %all_gather.37 = bf16[1024,256]{1,0:T(8,128)(2,1)S(1)} all-gather(bf16[128,256]{1,0:T(8,128)(2,1)} %param.20), channel_id=1, replica_groups=mesh['dp'=8,'tensor'=4] {'dp'}, dimensions={0}, use_global_device_ids=true | all-gather | bytes 589824 | tf_op jit(solution)/shard_map/all_gather | solution.py:168
  148.9 27.3 %all_gather.39 = bf16[256,1024]{1,0:T(8,128)(2,1)S(1)} all-gather(bf16[256,128]{1,0:T(8,128)(2,1)} %param.25), channel_id=1, replica_groups=mesh['dp'=8,'tensor'=4] {'dp'}, dimensions={1}, use_global_device_ids=true | all-gather | bytes 589824 | tf_op jit(solution)/shard_map/all_gather | solution.py:173
  198.3 16.9 %all-gather.1 = bf16[8,1,128]{2,1,0:T(2,128)(2,1)S(1)} all-gather(bf16[1,1,128]{2,1,0:T(2,128)(2,1)} %bitcast.205), channel_id=1, replica_groups=mesh['dp'=8,'tensor'=4] {'dp'}, dimensions={0}, use_global_device_ids=true | all-gather | bytes 2304 | tf_op jit(solution)/shard_map/all_gather | solution.py:206
  215.8 63.6 %all-reduce.19.cloned.1.call-done = f32[1024,1024]{1,0:T(8,128)} async-done(((f32[1024,1024]{1,0:T(8,128)}), f32[1024,1024]{1,0:T(8,128)}) %all-reduce.19.cloned.1.call-update) | async-done | bytes 4194320 | tf_op jit(solution)/shard_map/psum | solution.py:213
  286.7 7.3 fusion.82
  294.0 7.1 all-gather.6.cloned.1.call-done
  301.0 7.4 fusion.81
  308.4 47.0 %all-gather.10.cloned.1.call-done = bf16[1152,1024]{1,0:T(8,128)(2,1)} async-done(((bf16[1152,128]{1,0:T(8,128)(2,1)}), bf16[1152,1024]{1,0:T(8,128)(2,1)}) %all-gather.10.cloned.1.call-update) | async-done | bytes 2359312 | tf_op jit(solution)/shard_map/all_gather | solution.py:209
  355.4 10.9 multiply_convert_fusion
  369.7 4.4 convolution_add_fusion
  377.0 81.0 %all-reduce.21.cloned.1.call-done = f32[1024,1024]{1,0:T(8,128)} async-done(((f32[1024,1024]{1,0:T(8,128)}), f32[1024,1024]{1,0:T(8,128)}) %all-reduce.21.cloned.1.call-update) | async-done | bytes 4194320 | tf_op jit(solution)/shard_map/psum | solution.py:239
  458.0 5.2 multiply_reduce_fusion
  490.5 6.6 convolution_convert_fusion
  500.6 3.9 fusion.55
  506.4 7.2 fusion.91
  515.3 6.5 fusion.90
  521.9 6.2 fusion.89
  529.6 46.7 %all-reduce.23.cloned.1.call-done = f32[1024,1024]{1,0:T(8,128)} async-done(((f32[1024,1024]{1,0:T(8,128)}), f32[1024,1024]{1,0:T(8,128)}) %all-reduce.23.cloned.1.call-update) | async-done | bytes 4194320 | tf_op jit(solution)/shard_map/psum | solution.py:264
  579.8 21.9 %all-reduce.12 = (f32[1024]{0:T(1024)S(1)}, f32[64]{0:T(128)S(1)}, f32[64]{0:T(128)S(1)}, f32[1024]{0:T(1024)S(1)}) all-reduce(f32[1024]{0:T(1024)S(1)} %get-tuple-element.56, f32[64]{0:T(128)S(1)} %get-tuple-element.68, f32[64]{0:T(128)S(1)} %get-tuple-element.70, ...), channel_id=3, replica_groups=mesh['dp'=8,'tensor'=4] {'dp'}, use_global_device_ids=true, to_apply=%region_19.20.clone | all-reduce | flops 2176 | bytes 17408
  601.9 6.7 all-reduce.13
  612.9 5.4 fusion.14
  618.2 58.0 %reduce-scatter.15.cloned.1.call-done = f32[128,128]{1,0:T(8,128)} async-done(((f32[1024,128]{1,0:T(8,128)}), f32[128,128]{1,0:T(8,128)}) %reduce-scatter.15.cloned.1.call-update) | async-done | bytes 65552 | tf_op jit(solution)/shard_map/reduce_scatter | solution.py:279
  676.2 65.1 %reduce-scatter.13.cloned.1.call-done = f32[128,128]{1,0:T(8,128)} async-done(((f32[1024,128]{1,0:T(8,128)}), f32[128,128]{1,0:T(8,128)}) %reduce-scatter.13.cloned.1.call-update) | async-done | bytes 65552 | tf_op jit(solution)/shard_map/reduce_scatter | solution.py:278
  741.3 67.0 %reduce-scatter.17.cloned.1.call-done = f32[256,128]{1,0:T(8,128)} async-done(((f32[256,1024]{1,0:T(8,128)}), f32[256,128]{1,0:T(8,128)}) %reduce-scatter.17.cloned.1.call-update) | async-done | bytes 131088 | tf_op jit(solution)/shard_map/reduce_scatter | solution.py:282
  808.3 66.9 %reduce-scatter.11.cloned.1.call-done = f32[128,256]{1,0:T(8,128)} async-done(((f32[1024,256]{1,0:T(8,128)}), f32[128,256]{1,0:T(8,128)}) %reduce-scatter.11.cloned.1.call-update) | async-done | bytes 131088 | tf_op jit(solution)/shard_map/reduce_scatter | solution.py:277
  875.2 98.9 %reduce-scatter.23.cloned.1.call-done = f32[1152,128]{1,0:T(8,128)} async-done(((f32[1152,1024]{1,0:T(8,128)}), f32[1152,128]{1,0:T(8,128)}) %reduce-scatter.23.cloned.1.call-update) | async-done | bytes 589840 | tf_op jit(solution)/shard_map/reduce_scatter | solution.py:273
  974.1 99.1 %reduce-scatter.21.cloned.1.call-done = f32[128,1152]{1,0:T(8,128)} async-done(((f32[1024,1152]{1,0:T(8,128)}), f32[128,1152]{1,0:T(8,128)}) %reduce-scatter.21.cloned.1.call-update) | async-done | bytes 589840 | tf_op jit(solution)/shard_map/reduce_scatter | solution.py:272
  1073.2 99.2 %reduce-scatter.19.cloned.1.call-done = f32[128,1152]{1,0:T(8,128)} async-done(((f32[1024,1152]{1,0:T(8,128)}), f32[128,1152]{1,0:T(8,128)}) %reduce-scatter.19.cloned.1.call-update) | async-done | bytes 589840 | tf_op jit(solution)/shard_map/reduce_scatter | solution.py:271
  (261 shorter events, 84.3 us)
Async XLA Ops:
  8.0 271.4 %all-reduce.19.cloned.1.call-start = ((), (), s32[]{:S(2)}) async-start(), calls=%async_computation.8 | async-start | bytes 8388608 | tf_op jit(solution)/shard_map/psum | solution.py:213
  34.9 141.3 %copy-start.6 = (bf16[1024,1024]{1,0:T(8,128)(2,1)S(1)}, bf16[1024,1024]{1,0:T(8,128)(2,1)}, u32[]{:S(2)}) copy-start(bf16[1024,1024]{1,0:T(8,128)(2,1)} %param.15) | copy-start | bytes 6291460
  34.9 146.4 %copy-start.65 = (f32[64]{0:T(128)}, f32[64]{0:T(128)S(1)}, u32[]{:S(2)}) copy-start(f32[64]{0:T(128)S(1)} %convert_element_type.112) | copy-start | bytes 772
  34.9 146.2 %copy-start.63 = (f32[64]{0:T(128)}, f32[64]{0:T(128)S(1)}, u32[]{:S(2)}) copy-start(f32[64]{0:T(128)S(1)} %convert_element_type.110) | copy-start | bytes 772
  37.2 48.9 %copy-start.53 = (f32[1024]{0:T(1024)}, f32[1024]{0:T(1024)S(1)}, u32[]{:S(2)}) copy-start(f32[1024]{0:T(1024)S(1)} %fusion.17) | copy-start | bytes 12292
  37.2 140.4 %copy-start.49 = (f32[1024]{0:T(1024)}, f32[1024]{0:T(1024)S(1)}, u32[]{:S(2)}) copy-start(f32[1024]{0:T(1024)S(1)} %fusion.69) | copy-start | bytes 12292
  54.3 123.3 %copy-start.51 = (f32[8,1,128]{2,1,0:T(1,128)}, f32[8,1,128]{2,1,0:T(1,128)S(1)}, u32[]{:S(2)}) copy-start(f32[8,1,128]{2,1,0:T(1,128)S(1)} %convert_element_type.137) | copy-start | bytes 12292
  54.3 123.3 %copy-start.60 = (s32[1024]{0:T(1024)}, s32[1024]{0:T(1024)S(1)}, u32[]{:S(2)}) copy-start(s32[1024]{0:T(1024)S(1)} %iota.20) | copy-start | bytes 12292
  86.1 91.6 %copy-start.23 = (bf16[1024,128]{1,0:T(8,128)(2,1)}, bf16[1024,128]{1,0:T(8,128)(2,1)S(1)}, u32[]{:S(2)}) copy-start(bf16[1024,128]{1,0:T(8,128)(2,1)S(1)} %all_gather.35) | copy-start | bytes 786436
  117.2 61.3 %copy-start.19 = (bf16[1024,128]{1,0:T(8,128)(2,1)}, bf16[1024,128]{1,0:T(8,128)(2,1)S(1)}, u32[]{:S(2)}) copy-start(bf16[1024,128]{1,0:T(8,128)(2,1)S(1)} %all_gather.34) | copy-start | bytes 786436
  148.9 30.2 %copy-start.13 = (bf16[1024,256]{1,0:T(8,128)(2,1)}, bf16[1024,256]{1,0:T(8,128)(2,1)S(1)}, u32[]{:S(2)}) copy-start(bf16[1024,256]{1,0:T(8,128)(2,1)S(1)} %all_gather.37) | copy-start | bytes 1572868
  176.2 16.7 %copy-start.15 = (bf16[256,1024]{1,0:T(8,128)(2,1)}, bf16[256,1024]{1,0:T(8,128)(2,1)S(1)}, u32[]{:S(2)}) copy-start(bf16[256,1024]{1,0:T(8,128)(2,1)S(1)} %all_gather.39) | copy-start | bytes 1572868
  177.6 11.5 copy-start.30
  196.5 90.2 %all-gather.8.cloned.1.call-start = ((), (), s32[]{:S(2)}) async-start(), calls=%async_computation.10 | async-start | bytes 2654208 | tf_op jit(solution)/shard_map/all_gather | solution.py:208
  197.1 104.0 %all-gather.6.cloned.1.call-start = ((), (), s32[]{:S(2)}) async-start(), calls=%async_computation.9 | async-start | bytes 2654208 | tf_op jit(solution)/shard_map/all_gather | solution.py:207
  197.7 157.7 %all-gather.10.cloned.1.call-start = ((), (), s32[]{:S(2)}) async-start(), calls=%async_computation.11 | async-start | bytes 2654208 | tf_op jit(solution)/shard_map/all_gather | solution.py:209
  198.2 259.8 %all-reduce.21.cloned.1.call-start = ((), (), s32[]{:S(2)}) async-start(), calls=%async_computation.13 | async-start | bytes 8388608 | tf_op jit(solution)/shard_map/psum | solution.py:239
  355.4 11.0 copy-start.68
  374.2 202.1 %all-reduce.23.cloned.1.call-start = ((), (), s32[]{:S(2)}) async-start(), calls=%async_computation.14 | async-start | bytes 8388608 | tf_op jit(solution)/shard_map/psum | solution.py:264
  490.5 120.1 %reduce-scatter.9.cloned.1.call-start = ((), (), s32[]{:S(2)}) async-start(), calls=%async_computation.12 | async-start | bytes 2621440 | tf_op jit(solution)/shard_map/reduce_scatter | solution.py:221
  497.2 179.0 %reduce-scatter.15.cloned.1.call-start = ((), (), s32[]{:S(2)}) async-start(), calls=%async_computation.17 | async-start | bytes 589824 | tf_op jit(solution)/shard_map/reduce_scatter | solution.py:279
  498.9 242.5 %reduce-scatter.13.cloned.1.call-start = ((), (), s32[]{:S(2)}) async-start(), calls=%async_computation.16 | async-start | bytes 589824 | tf_op jit(solution)/shard_map/reduce_scatter | solution.py:278
  500.5 307.8 %reduce-scatter.17.cloned.1.call-start = ((), (), s32[]{:S(2)}) async-start(), calls=%async_computation.18 | async-start | bytes 1179648 | tf_op jit(solution)/shard_map/reduce_scatter | solution.py:282
  504.5 370.7 %reduce-scatter.11.cloned.1.call-start = ((), (), s32[]{:S(2)}) async-start(), calls=%async_computation.15 | async-start | bytes 1179648 | tf_op jit(solution)/shard_map/reduce_scatter | solution.py:277
  506.4 467.8 %reduce-scatter.23.cloned.1.call-start = ((), (), s32[]{:S(2)}) async-start(), calls=%async_computation.21 | async-start | bytes 5308416 | tf_op jit(solution)/shard_map/reduce_scatter | solution.py:273
  513.7 559.6 %reduce-scatter.21.cloned.1.call-start = ((), (), s32[]{:S(2)}) async-start(), calls=%async_computation.20 | async-start | bytes 5308416 | tf_op jit(solution)/shard_map/reduce_scatter | solution.py:272
  521.8 650.7 %reduce-scatter.19.cloned.1.call-start = ((), (), s32[]{:S(2)}) async-start(), calls=%async_computation.19 | async-start | bytes 5308416 | tf_op jit(solution)/shard_map/reduce_scatter | solution.py:271
  528.1 48.1 %copy-start.7 = (bf16[1024,1024]{1,0:T(8,128)(2,1)S(1)}, bf16[1024,1024]{1,0:T(8,128)(2,1)}, u32[]{:S(2)}) copy-start(bf16[1024,1024]{1,0:T(8,128)(2,1)} %param.15) | copy-start | bytes 6291460
  528.1 48.2 %copy-start.50 = (f32[1024]{0:T(1024)S(1)}, f32[1024]{0:T(1024)}, u32[]{:S(2)}) copy-start(f32[1024]{0:T(1024)} %copy-done.49) | copy-start | bytes 12292
  528.1 48.2 %copy-start.52 = (f32[8,1,128]{2,1,0:T(1,128)S(1)}, f32[8,1,128]{2,1,0:T(1,128)}, u32[]{:S(2)}) copy-start(f32[8,1,128]{2,1,0:T(1,128)} %copy-done.51) | copy-start | bytes 12292
  528.1 51.7 %copy-start.62 = (f32[1024]{0:T(1024)S(1)}, f32[1024]{0:T(1024)}, u32[]{:S(2)}) copy-start(f32[1024]{0:T(1024)} %get-tuple-element.54) | copy-start | bytes 12292
  528.1 81.6 %copy-start.54 = (f32[1024]{0:T(1024)S(1)}, f32[1024]{0:T(1024)}, u32[]{:S(2)}) copy-start(f32[1024]{0:T(1024)} %copy-done.53) | copy-start | bytes 12292
  (56 other events, 162.2 us)
Sparse Core Ops, SparseCore 0:
  196.6 82.7 all-reduce.18
  374.3 83.6 all-reduce.20
  490.6 85.6 all-reduce.22
  578.8 31.7 reduce-scatter.8
  614.3 61.8 reduce-scatter.14
  680.3 60.9 reduce-scatter.12
  745.3 62.9 reduce-scatter.16
  812.7 62.4 reduce-scatter.10
  879.4 94.6 reduce-scatter.22
  978.2 94.9 reduce-scatter.20
  1077.5 94.9 reduce-scatter.18
Sparse Core Ops, SparseCore 1:
  199.4 49.0 all-gather.7
  250.7 50.3 all-gather.5
  303.2 52.2 all-gather.9
where the time goes:
time: 1190 us; the launch traced here: 1180 us
  waiting for transfers between devices  802 us (67%)
  blocking collectives  206 us (17%)
  matrix products  91.8 us (8%)
  other arithmetic  40 us (3%)
  local copies, waits for them, and re-layouts  20.4 us (2%)
  between operations  19.2 us (2%)
    reduce_scatter x1, waiting for transfers between devices, body(): lax.psum_scatter(gate_grad, 'dp', scatter_dimension=0, tiled=True)  99.2 us
    reduce_scatter x1, waiting for transfers between devices, body(): lax.psum_scatter(up_grad, 'dp', scatter_dimension=0, tiled=True)  99.1 us
    reduce_scatter x1, waiting for transfers between devices, body(): lax.psum_scatter(down_grad, 'dp', scatter_dimension=1, tiled=True)  98.9 us
    psum x1, waiting for transfers between devices, body(): lax.psum(ffn_input_part, 'tensor')  81 us
    reduce_scatter x1, waiting for transfers between devices, body(): lax.psum_scatter(out_grad, 'dp', scatter_dimension=1, tiled=True)  67 us
    reduce_scatter x1, waiting for transfers between devices, body(): lax.psum_scatter(query_weight_grad, 'dp', scatter_dimension=0, tiled=True)  66.9 us
    reduce_scatter x1, waiting for transfers between devices, body(): lax.psum_scatter(key_weight_grad, 'dp', scatter_dimension=0, tiled=True)  65.1 us
    psum x1, waiting for transfers between devices, body(): residual = inputs + lax.psum(attn_part, 'tensor')  63.6 us
  transfers between devices with their start and end apart: 14, of which 13 were waited for; matrix products, arithmetic and copies ran while one was open for 6% of the time, Pallas kernels for 0%

commit v1 on v0

--- a/solution.py
+++ b/solution.py
@@ -1,6 +1,10 @@
+import functools
+
 import jax
 import jax.numpy as jnp
 from jax import lax
+from jax.experimental import pallas as pl
+from jax.experimental.pallas import tpu as pltpu
 from jax.sharding import PartitionSpec as P
 
 HD = 64
@@ -140,6 +144,327 @@
         key_total = key_total + jnp.pad(key_part, padding)
         value_total = value_total + jnp.pad(value_part, padding)
     return (jnp.concatenate(query_pieces, axis=0), key_total, value_total)
+
+
+MESH = pl.DeviceIdType.MESH
+VMEM_BYTES = 44 * 1024 * 1024
+
+
+def block_of(ref, place, size):
+    return ref.at[pl.ds(pl.multiple_of(place * size, size), size), :]
+
+
+def greet(peers):
+    barrier = pltpu.get_barrier_semaphore()
+    for peer in peers:
+        pl.semaphore_signal(barrier, inc=1, device_id=peer, device_id_type=MESH)
+    pl.semaphore_wait(barrier, len(peers))
+
+
+def dp_places(size):
+    me = lax.axis_index("dp")
+    return me // 2, lax.rem(me, 2), size // 2
+
+
+def gather_kernel(size, count, *refs):
+    shards, wholes = refs[:count], refs[count : 2 * count]
+    own_sem, far_send, far_recv, near_send, near_recv = refs[2 * count :]
+    column, side, columns = dp_places(size)
+    near = {"dp": column * 2 + 1 - side}
+    far = [{"dp": lax.rem(column + k, columns) * 2 + side} for k in range(1, columns)]
+    greet([near] + far)
+    mine = column * 2 + side
+    started = []
+
+    def slot(a, place):
+        return block_of(wholes[a], place, shards[a].shape[0])
+
+    for a in range(count):
+        own = pltpu.make_async_copy(shards[a], slot(a, mine), own_sem.at[a])
+        own.start()
+        started.append(own.wait)
+        copy = pltpu.make_async_remote_copy(
+            src_ref=shards[a], dst_ref=slot(a, mine),
+            send_sem=near_send.at[a, 0], recv_sem=near_recv.at[a, 0],
+            device_id=near, device_id_type=MESH,
+        )
+        copy.start()
+        started.append(copy.wait)
+    arrivals = []
+    for k in range(1, columns):
+        for a in range(count):
+            copy = pltpu.make_async_remote_copy(
+                src_ref=shards[a], dst_ref=slot(a, mine),
+                send_sem=far_send.at[a, k - 1], recv_sem=far_recv.at[a, k - 1],
+                device_id=far[k - 1], device_id_type=MESH,
+            )
+            copy.start()
+            started.append(copy.wait_send)
+            arrivals.append((k, a))
+    for k, a in arrivals:
+        place = lax.rem(column + columns - k, columns) * 2 + side
+        landed = pltpu.make_async_remote_copy(
+            src_ref=shards[a], dst_ref=slot(a, place),
+            send_sem=far_send.at[a, k - 1], recv_sem=far_recv.at[a, k - 1],
+            device_id=near, device_id_type=MESH,
+        )
+        landed.wait_recv()
+        copy = pltpu.make_async_remote_copy(
+            src_ref=slot(a, place), dst_ref=slot(a, place),
+            send_sem=near_send.at[a, k], recv_sem=near_recv.at[a, k],
+            device_id=near, device_id_type=MESH,
+        )
+        copy.start()
+        started.append(copy.wait)
+    for wait in started:
+        wait()
+
+
+def gather_dp(arrays, collective_id):
+    size = lax.axis_size("dp")
+    columns, count = size // 2, len(arrays)
+    shapes = [
+        jax.ShapeDtypeStruct((size * array.shape[0], array.shape[1]), array.dtype)
+        for array in arrays
+    ]
+    dma = pltpu.SemaphoreType.DMA
+    return pl.pallas_call(
+        functools.partial(gather_kernel, size, count),
+        out_shape=tuple(shapes),
+        in_specs=[pl.BlockSpec(memory_space=pl.ANY)] * count,
+        out_specs=tuple([pl.BlockSpec(memory_space=pl.ANY)] * count),
+        scratch_shapes=[
+            dma((count,)),
+            dma((count, columns - 1)),
+            dma((count, columns - 1)),
+            dma((count, columns)),
+            dma((count, columns)),
+        ],
+        compiler_params=pltpu.CompilerParams(collective_id=collective_id, has_side_effects=True),
+    )(*arrays)
+
+
+def scatter_kernel(size, count, *refs):
+    parts, sums = refs[:count], refs[count : 2 * count]
+    near_slots = refs[2 * count : 3 * count]
+    leaving = refs[3 * count : 4 * count]
+    far_slots = refs[4 * count : 5 * count]
+    near_send, near_recv, far_send, far_recv = refs[5 * count :]
+    column, side, columns = dp_places(size)
+    near = {"dp": column * 2 + 1 - side}
+    far = [{"dp": lax.rem(column + k, columns) * 2 + side} for k in range(1, columns)]
+    greet([near] + far)
+    order = [(k, a) for k in list(range(1, columns)) + [0] for a in range(count)]
+
+    def part(a, place):
+        return block_of(parts[a], place, sums[a].shape[0])
+
+    near_copies, far_copies = {}, {}
+    for k, a in order:
+        place = lax.rem(column + k, columns) * 2 + 1 - side
+        copy = pltpu.make_async_remote_copy(
+            src_ref=part(a, place), dst_ref=near_slots[a].at[k],
+            send_sem=near_send.at[a, k], recv_sem=near_recv.at[a, k],
+            device_id=near, device_id_type=MESH,
+        )
+        copy.start()
+        near_copies[k, a] = copy
+    for k, a in order:
+        near_copies[k, a].wait_recv()
+        place = lax.rem(column + k, columns) * 2 + side
+        total = part(a, place)[...].astype(jnp.float32) + near_slots[a][k].astype(jnp.float32)
+        if k == 0:
+            sums[a][...] = total
+            continue
+        leaving[a][k - 1] = total.astype(jnp.bfloat16)
+        copy = pltpu.make_async_remote_copy(
+            src_ref=leaving[a].at[k - 1], dst_ref=far_slots[a].at[k - 1],
+            send_sem=far_send.at[a, k - 1], recv_sem=far_recv.at[a, k - 1],
+            device_id=far[k - 1], device_id_type=MESH,
+        )
+        copy.start()
+        far_copies[k, a] = copy
+    for k, a in order:
+        if k > 0:
+            far_copies[k, a].wait_recv()
+            sums[a][...] += far_slots[a][k - 1].astype(jnp.float32)
+    for k, a in order:
+        near_copies[k, a].wait_send()
+        if k > 0:
+            far_copies[k, a].wait_send()
+
+
+def scatter_dp(arrays, collective_id):
+    size = lax.axis_size("dp")
+    columns, count = size // 2, len(arrays)
+    shapes = [(array.shape[0] // size, array.shape[1]) for array in arrays]
+    dma = pltpu.SemaphoreType.DMA
+    return pl.pallas_call(
+        functools.partial(scatter_kernel, size, count),
+        out_shape=tuple(jax.ShapeDtypeStruct(shape, jnp.float32) for shape in shapes),
+        in_specs=[pl.BlockSpec(memory_space=pltpu.VMEM)] * count,
+        out_specs=tuple([pl.BlockSpec(memory_space=pltpu.VMEM)] * count),
+        scratch_shapes=[pltpu.VMEM((columns,) + shape, jnp.bfloat16) for shape in shapes]
+        + [pltpu.VMEM((columns - 1,) + shape, jnp.bfloat16) for shape in shapes]
+        + [pltpu.VMEM((columns - 1,) + shape, jnp.bfloat16) for shape in shapes]
+        + [
+            dma((count, columns)),
+            dma((count, columns)),
+            dma((count, columns - 1)),
+            dma((count, columns - 1)),
+        ],
+        compiler_params=pltpu.CompilerParams(
+            collective_id=collective_id, has_side_effects=True, vmem_limit_bytes=VMEM_BYTES
+        ),
+    )(*arrays)
+
+
+def total_kernel(size, *refs):
+    (part, small, whole, small_sum, near_slots, leaving, far_slots, small_slots,
+     near_send, near_recv, far_send, far_recv, back_send, back_recv, on_send, on_recv,
+     small_send, small_recv) = refs
+    me = lax.axis_index("tensor")
+    column, side, columns = me // 2, lax.rem(me, 2), size // 2
+    share = whole.shape[0] // size
+    near = {"tensor": column * 2 + 1 - side}
+    far = [{"tensor": lax.rem(column + k, columns) * 2 + side} for k in range(1, columns)]
+    others = [{"tensor": lax.rem(me + k, size)} for k in range(1, size)]
+    greet(others)
+
+    def rows(ref, place):
+        return block_of(ref, place, share)
+
+    small_copies = []
+    for k in range(1, size):
+        copy = pltpu.make_async_remote_copy(
+            src_ref=small, dst_ref=small_slots.at[k - 1],
+            send_sem=small_send.at[k - 1], recv_sem=small_recv.at[k - 1],
+            device_id=others[k - 1], device_id_type=MESH,
+        )
+        small_copies.append(copy)
+    near_copies, far_copies, started = [], [], []
+    order = list(range(1, columns)) + [0]
+    for k in order:
+        place = lax.rem(column + k, columns) * 2 + 1 - side
+        copy = pltpu.make_async_remote_copy(
+            src_ref=rows(part, place), dst_ref=near_slots.at[k],
+            send_sem=near_send.at[k], recv_sem=near_recv.at[k],
+            device_id=near, device_id_type=MESH,
+        )
+        copy.start()
+        near_copies.append(copy)
+    for copy in small_copies:
+        copy.start()
+    mine = rows(whole, me)
+    for k, arrived in zip(order, near_copies):
+        arrived.wait_recv()
+        place = lax.rem(column + k, columns) * 2 + side
+        total = rows(part, place)[...].astype(jnp.float32) + near_slots[k].astype(jnp.float32)
+        if k > 0:
+            leaving[k - 1] = total.astype(jnp.bfloat16)
+            copy = pltpu.make_async_remote_copy(
+                src_ref=leaving.at[k - 1], dst_ref=far_slots.at[k - 1],
+                send_sem=far_send.at[k - 1], recv_sem=far_recv.at[k - 1],
+                device_id=far[k - 1], device_id_type=MESH,
+            )
+            copy.start()
+            far_copies.append(copy)
+    for copy in far_copies:
+        copy.wait_recv()
+    for k in range(1, columns):
+        total = total + far_slots[k - 1].astype(jnp.float32)
+    mine[...] = total.astype(jnp.bfloat16)
+    for k in range(1, columns):
+        copy = pltpu.make_async_remote_copy(
+            src_ref=mine, dst_ref=rows(whole, me),
+            send_sem=back_send.at[k - 1], recv_sem=back_recv.at[k - 1],
+            device_id=far[k - 1], device_id_type=MESH,
+        )
+        copy.start()
+        started.append(copy.wait_send)
+    copy = pltpu.make_async_remote_copy(
+        src_ref=mine, dst_ref=rows(whole, me),
+        send_sem=on_send.at[0], recv_sem=on_recv.at[0],
+        device_id=near, device_id_type=MESH,
+    )
+    copy.start()
+    started.append(copy.wait)
+    for copy in small_copies:
+        copy.wait_recv()
+    small_total = small[...]
+    for k in range(1, size):
+        small_total = small_total + small_slots[k - 1]
+    small_sum[...] = small_total
+    for k in range(1, columns):
+        place = lax.rem(column + columns - k, columns) * 2 + side
+        landed = pltpu.make_async_remote_copy(
+            src_ref=mine, dst_ref=rows(whole, place),
+            send_sem=back_send.at[k - 1], recv_sem=back_recv.at[k - 1],
+            device_id=near, device_id_type=MESH,
+        )
+        landed.wait_recv()
+        copy = pltpu.make_async_remote_copy(
+            src_ref=rows(whole, place), dst_ref=rows(whole, place),
+            send_sem=on_send.at[k], recv_sem=on_recv.at[k],
+            device_id=near, device_id_type=MESH,
+        )
+        copy.start()
+        started.append(copy.wait)
+    for wait in started:
+        wait()
+    for copy in near_copies + far_copies + small_copies:
+        copy.wait_send()
+
+
+def total_tensor(part, small, collective_id):
+    size = lax.axis_size("tensor")
+    columns = size // 2
+    length, width = part.shape
+    share = length // size
+    dma = pltpu.SemaphoreType.DMA
+    return pl.pallas_call(
+        functools.partial(total_kernel, size),
+        out_shape=(
+            jax.ShapeDtypeStruct(part.shape, jnp.bfloat16),
+            jax.ShapeDtypeStruct(small.shape, jnp.float32),
+        ),
+        in_specs=[pl.BlockSpec(memory_space=pltpu.VMEM)] * 2,
+        out_specs=tuple([pl.BlockSpec(memory_space=pltpu.VMEM)] * 2),
+        scratch_shapes=[
+            pltpu.VMEM((columns, share, width), jnp.bfloat16),
+            pltpu.VMEM((columns - 1, share, width), jnp.bfloat16),
+            pltpu.VMEM((columns - 1, share, width), jnp.bfloat16),
+            pltpu.VMEM((size - 1,) + small.shape, jnp.float32),
+            dma((columns,)),
+            dma((columns,)),
+            dma((columns - 1,)),
+            dma((columns - 1,)),
+            dma((columns - 1,)),
+            dma((columns - 1,)),
+            dma((columns,)),
+            dma((columns,)),
+            dma((size - 1,)),
+            dma((size - 1,)),
+        ],
+        compiler_params=pltpu.CompilerParams(
+            collective_id=collective_id, has_side_effects=True, vmem_limit_bytes=VMEM_BYTES
+        ),
+    )(part, small)
+
+
+def pack_rows(rows):
+    padded = [jnp.pad(row, (0, 128 - row.shape[0])) for row in rows]
+    padded = padded + [jnp.zeros_like(padded[0])] * (16 - len(padded))
+    return jnp.stack(padded)
+
+
+def pack_sums(vectors, size):
+    blocks = []
+    for vector in vectors:
+        share = vector.reshape(size, -1)
+        blocks.append(jnp.pad(share, ((0, 0), (0, 128 - share.shape[1]))))
+    blocks = blocks + [jnp.zeros_like(blocks[0])] * (16 - len(blocks))
+    return jnp.stack(blocks, axis=1).reshape(size * 16, 128).astype(jnp.bfloat16)
 
 
 def swiglu(gate_in, up_in):
@@ -163,16 +488,17 @@
     w_up,
     w_down,
 ):
-    attn_set = (
-        lax.all_gather(attn_gain, "dp", axis=0, tiled=True),
-        lax.all_gather(w_query, "dp", axis=0, tiled=True),
-        lax.all_gather(w_key, "dp", axis=0, tiled=True),
-        lax.all_gather(w_value, "dp", axis=0, tiled=True),
-        lax.all_gather(query_gain, "dp", axis=0, tiled=True),
-        lax.all_gather(key_gain, "dp", axis=0, tiled=True),
-        lax.all_gather(w_out, "dp", axis=1, tiled=True),
-    )
-    gain_first, query_full, key_full, value_full, qgain_full, kgain_full, out_full = attn_set
+    dp_size = lax.axis_size("dp")
+    gain_tile = pack_rows([attn_gain, ffn_gain, query_gain, key_gain])
+    gain_tiles, query_full, key_full, value_full, out_full = gather_dp(
+        (gain_tile, w_query, w_key, w_value, w_out.T), 1
+    )
+    gain_tiles = gain_tiles.reshape(dp_size, 16, 128)
+    gain_first = gain_tiles[:, 0, : attn_gain.shape[0]].reshape(-1)
+    gain_second = gain_tiles[:, 1, : ffn_gain.shape[0]].reshape(-1)
+    qgain_full = gain_tiles[:, 2, : query_gain.shape[0]].reshape(-1)
+    kgain_full = gain_tiles[:, 3, : key_gain.shape[0]].reshape(-1)
+    no_small = jnp.zeros((8, 128), jnp.float32)
     token_count = tokens.shape[0]
     seq_count = token_count // LEN
     local_heads = query_full.shape[1] // HD
@@ -201,16 +527,11 @@
     seq_segments = segments.reshape(seq_count, LEN)
     mixed, lse_rows = lax.map(attend, (query_low, key_low, value_low, seq_segments))
     mixed_low = mixed.reshape(token_count, local_heads * HD).astype(jnp.bfloat16)
-    attn_part = matmul(mixed_low, out_full)
-    ffn_set = (
-        lax.all_gather(ffn_gain, "dp", axis=0, tiled=True),
-        lax.all_gather(w_gate, "dp", axis=0, tiled=True),
-        lax.all_gather(w_up, "dp", axis=0, tiled=True),
-        lax.all_gather(w_down, "dp", axis=1, tiled=True),
-    )
-    gain_second, gate_full, up_full, down_full = ffn_set
+    attn_part = matmul_nt(mixed_low, out_full).astype(jnp.bfloat16)
+    gate_full, up_full, down_full = gather_dp((w_gate, w_up, w_down.T), 2)
     ffn_scale = gain_second.astype(jnp.float32)
-    residual = inputs + lax.psum(attn_part, "tensor")
+    attn_total, _ = total_tensor(attn_part, no_small, 3)
+    residual = inputs + attn_total.astype(jnp.float32)
     ffn_float, ffn_norm_back = jax.vjp(norm_rows, residual, ffn_scale)
     normed_ffn = ffn_float.astype(jnp.bfloat16)
     residual_rows = lax.dynamic_slice_in_dim(residual, own_start, share_rows, 0)
@@ -219,7 +540,7 @@
     hidden_float, swiglu_back = jax.vjp(swiglu, gate_value, up_value)
     hidden = hidden_float.astype(jnp.bfloat16)
     ffn_share = lax.psum_scatter(
-        matmul(
+        matmul_nt(
             lax.slice_in_dim(hidden, 0, share_rows * lax.axis_size("tensor"), axis=0), down_full
         ).astype(jnp.bfloat16),
         "tensor",
@@ -228,20 +549,21 @@
     ).astype(jnp.float32)
     output = (residual_rows + ffn_share).astype(jnp.bfloat16)
     grad_output = cotangent.astype(jnp.float32)
-    down_grad = matmul_tn(hidden, cotangent)
-    grad_hidden = matmul_nt(cotangent, down_full)
+    down_grad = matmul_tn(cotangent, hidden)
+    grad_hidden = matmul(cotangent, down_full)
     grad_gate, grad_up = swiglu_back(grad_hidden)
     gate_low = grad_gate.astype(jnp.bfloat16)
     up_low = grad_up.astype(jnp.bfloat16)
     gate_grad = matmul_tn(normed_ffn, gate_low)
     up_grad = matmul_tn(normed_ffn, up_low)
     ffn_input_part = matmul_nt(gate_low, gate_full) + matmul_nt(up_low, up_full)
-    residual_part, ffn_gain_part = ffn_norm_back(lax.psum(ffn_input_part, "tensor"))
+    ffn_input_grad, _ = total_tensor(ffn_input_part.astype(jnp.bfloat16), no_small, 4)
+    residual_part, ffn_gain_part = ffn_norm_back(ffn_input_grad.astype(jnp.float32))
     grad_residual = residual_part + grad_output
     grad_attn_low = grad_residual.astype(jnp.bfloat16)
-    out_grad = matmul_tn(mixed_low, grad_attn_low)
+    out_grad = matmul_tn(grad_attn_low, mixed_low)
     grad_mixed = (
-        matmul_nt(grad_attn_low, out_full)
+        matmul(grad_attn_low, out_full)
         .astype(jnp.bfloat16)
         .reshape(seq_count, LEN, local_kv, group_size, HD)
     )
@@ -261,40 +583,41 @@
         + matmul_nt(key_low_grad, key_full)
         + matmul_nt(value_low_grad, value_full)
     )
-    attn_input_grad, qgain_total, kgain_total = lax.psum(
-        (attn_input_part, grad_qgain, grad_kgain), "tensor"
-    )
-    input_part, attn_gain_grad = attn_norm_back(attn_input_grad)
+    gain_sums = jnp.pad(
+        jnp.stack([grad_qgain, grad_kgain]), ((0, 6), (0, 128 - grad_qgain.shape[0]))
+    )
+    attn_input_grad, gain_sums = total_tensor(attn_input_part.astype(jnp.bfloat16), gain_sums, 5)
+    qgain_total = gain_sums[0, : grad_qgain.shape[0]]
+    kgain_total = gain_sums[1, : grad_kgain.shape[0]]
+    input_part, attn_gain_grad = attn_norm_back(attn_input_grad.astype(jnp.float32))
     tokens_grad = input_part + grad_residual
-    ffn_grads = (
-        lax.psum_scatter(ffn_gain_part, "dp", scatter_dimension=0, tiled=True),
-        lax.psum_scatter(gate_grad, "dp", scatter_dimension=0, tiled=True),
-        lax.psum_scatter(up_grad, "dp", scatter_dimension=0, tiled=True),
-        lax.psum_scatter(down_grad, "dp", scatter_dimension=1, tiled=True),
-    )
-    attn_grads = (
-        lax.psum_scatter(attn_gain_grad, "dp", scatter_dimension=0, tiled=True),
-        lax.psum_scatter(query_weight_grad, "dp", scatter_dimension=0, tiled=True),
-        lax.psum_scatter(key_weight_grad, "dp", scatter_dimension=0, tiled=True),
-        lax.psum_scatter(value_weight_grad, "dp", scatter_dimension=0, tiled=True),
-        lax.psum_scatter(qgain_total, "dp", scatter_dimension=0, tiled=True),
-        lax.psum_scatter(kgain_total, "dp", scatter_dimension=0, tiled=True),
-        lax.psum_scatter(out_grad, "dp", scatter_dimension=1, tiled=True),
-    )
+    ffn_grads = scatter_dp(
+        [grad.astype(jnp.bfloat16) for grad in (gate_grad, up_grad, down_grad)], 6
+    )
+    gain_grads = pack_sums([attn_gain_grad, ffn_gain_part, qgain_total, kgain_total], dp_size)
+    attn_grads = scatter_dp(
+        [gain_grads]
+        + [
+            grad.astype(jnp.bfloat16)
+            for grad in (query_weight_grad, key_weight_grad, value_weight_grad, out_grad)
+        ],
+        7,
+    )
+    gain_grads = attn_grads[0]
     return (
         output,
         tokens_grad,
-        attn_grads[0],
+        gain_grads[0, : attn_gain.shape[0]],
         attn_grads[1],
         attn_grads[2],
         attn_grads[3],
-        attn_grads[4],
-        attn_grads[5],
-        attn_grads[6],
+        gain_grads[2, : query_gain.shape[0]],
+        gain_grads[3, : key_gain.shape[0]],
+        attn_grads[4].T,
+        gain_grads[1, : ffn_gain.shape[0]],
         ffn_grads[0],
         ffn_grads[1],
-        ffn_grads[2],
-        ffn_grads[3],
+        ffn_grads[2].T,
     )
 
 

time: 1190 us -> 510 us (0.43)
  waiting for transfers between devices: 802 us -> 0.02 us
  Pallas kernels: 0 us -> 354 us
  blocking collectives: 206 us -> 0 us
  matrix products: 91.8 us -> 70.2 us
    reduce_scatter x8 -> x1, waiting for transfers between devices: 555 us -> 0.01 us  [body(): lax.psum_scatter(matmul_nt(lax.slice_in_dim(hidden, 0, share_rows * lax.a...]
    pallas_call x0 -> x7, Pallas kernels: none -> 354 us  [the longest x2 135 us: scatter_dp(): pl.pallas_call(functools.partial(scatter_kernel, size, count), out_shape=...]
    psum x3 -> x0, waiting for transfers between devices: 191 us -> none  [the longest x1 81 us: body(): lax.psum(ffn_input_part, 'tensor')]
    all_gather x6 -> x0, blocking collectives: 154 us -> none  [the longest x1 31.7 us: body(): lax.all_gather(w_query, 'dp', axis=0, tiled=True)]
    all_gather x3 -> x0, waiting for transfers between devices: 54.1 us -> none  [the longest x1 47 us: body(): lax.all_gather(w_down, 'dp', axis=1, tiled=True)]
    unnamed x2 -> x0, blocking collectives: 45 us -> none
  transfers between devices with their start and end apart: 14 -> 1, of which waited for: 13 -> 0; matrix products, arithmetic and copies ran while one was open for 6% -> 13% of each run, Pallas kernels for 0% -> 40%
where the time goes in v1:
time: 510 us; the launch traced here: 501 us
  Pallas kernels  354 us (69%)
  matrix products  70.2 us (14%)
  other arithmetic  35.7 us (7%)
  local copies, waits for them, and re-layouts  25.3 us (5%)
  between operations  15.7 us (3%)
    pallas_call x2, Pallas kernels, scatter_dp(): pl.pallas_call(functools.partial(scatter_kernel, size, count), out_shape=...  135 us
    pallas_call x2, Pallas kernels, gather_dp(): pl.pallas_call(functools.partial(gather_kernel, size, count), out_shape=t...  121 us
    pallas_call x3, Pallas kernels, total_tensor(): pl.pallas_call(functools.partial(total_kernel, size), out_shape=(jax.Shap...  97.8 us
    unnamed x165, local copies, waits for them, and re-layouts  20.4 us
    dot_general x7, matrix products, matmul(): return jnp.dot(left, right, preferred_element_type=jnp.float32)  19.4 us
    dot_general x7, matrix products, matmul_tn(): lax.dot_general(left, right, (((0,), (0,)), ((), ())), preferred_element_...  17 us
    dot_general x7, matrix products, matmul_nt(): lax.dot_general(left, right, (((1,), (1,)), ((), ())), preferred_element_...  16.2 us
  transfers between devices with their start and end apart: 1, of which 0 were waited for; matrix products, arithmetic and copies ran while one was open for 13% of the time, Pallas kernels for 40%

profile of v1, /device:TPU:0, one launch (start us, length us, event | category | flops | bytes accessed | tf_op | source)
XLA Modules:
  0.0 500.9 jit_solution(4409142754053270144)
XLA Ops:
  9.5 1.9 stack.62.refs_0_
  11.3 28.4 %shard_map.246 = (bf16[128,128]{1,0:T(8,128)(2,1)}, bf16[1024,256]{1,0:T(8,128)(2,1)}, bf16[1024,128]{1,0:T(8,128)(2,1)}, bf16[1024,128]{1,0:T(8,128)(2,1)}, bf16[1024,256]{1,0:T(8,128)(2,1)}) custom-call(bf16[16,128]{1,0:T(8,128)(2,1)} %stack.62.refs_0_, bf16[128,256]{1,0:T(8,128)(2,1)} %refs_1_.2, bf16[128,128]{1,0:T(8,128)(2,1)} %refs_2_.1, ...), custom_call_target="tpu_custom_call" | custom-call | tf_op jit(solution)/shard_map/pallas_call | solution.py:231
  41.4 2.1 fusion.22
  43.5 2.1 fusion.14
  55.5 2.1 copy-done.4
  63.8 31.9 %shard_map.247 = (bf16[1024,1024]{1,0:T(8,128)(2,1)S(1)}, f32[8,128]{1,0:T(8,128)}) custom-call(bf16[1024,1024]{1,0:T(8,128)(2,1)S(1)} %convolution_convert_fusion.4.refs_0_, f32[8,128]{1,0:T(8,128)S(1)} %broadcast_in_dim.115.refs_1_), custom_call_target="tpu_custom_call" | custom-call | tf_op jit(solution)/shard_map/pallas_call | solution.py:425
  97.1 1.9 copy.51
  98.9 3.7 multiply_convert_fusion.1
  102.7 92.7 %shard_map.248 = (bf16[1024,1152]{1,0:T(8,128)(2,1)}, bf16[1024,1152]{1,0:T(8,128)(2,1)}, bf16[1024,1152]{1,0:T(8,128)(2,1)}) custom-call(bf16[128,1152]{1,0:T(8,128)(2,1)} %refs_0_.1, bf16[128,1152]{1,0:T(8,128)(2,1)} %refs_1_.3, bf16[128,1152]{1,0:T(8,128)(2,1)} %bitcast.238), custom_call_target="tpu_custom_call" | custom-call | tf_op jit(solution)/shard_map/pallas_call | solution.py:231
  195.4 5.3 %fusion.85 = f32[1024,1152]{1,0:T(8,128)S(1)} fusion(bf16[1024,1024]{1,0:T(8,128)(2,1)} %multiply_convert_fusion.1, bf16[1024,1152]{1,0:T(8,128)(2,1)} %get-tuple-element.90), kind=kOutput, calls=%fused_computation.181 | convolution fusion | flops 2415919104 | bytes 9175040 | tf_op jit(solution)/shard_map/dot_general | solution.py:44
  200.8 2.9 fusion.86
  203.7 6.2 %fusion.12 = (bf16[1024,1152]{1,0:T(8,128)(2,1)}, bf16[1024,1152]{1,0:T(8,128)(2,1)}, bf16[1024,1152]{1,0:T(8,128)(2,1)S(1)}) fusion(f32[1024,1152]{1,0:T(8,128)S(1)} %fusion.85, f32[1024,1152]{1,0:T(8,128)S(1)} %fusion.86, bf16[1024,1024]{1,0:T(8,128)(2,1)S(1)} %copy-done.17, bf16[1024,1152]{1,0:T(8,128)(2,1)S(1)} %copy-done.71), kind=kOutput, calls=%fused_computation.32 | convolution fusion | flops 2434793472 | bytes 20971520 | tf_op jit(solution)/shard_map/dot_general | solution.py:44
  211.3 4.1 convolution_convert_fusion.3
  217.0 5.4 %fusion.87 = f32[1024,1024]{1,0:T(8,128)S(1)} fusion(bf16[1024,1152]{1,0:T(8,128)(2,1)} %get-tuple-element.141, bf16[1024,1152]{1,0:T(8,128)(2,1)} %get-tuple-element.90), kind=kOutput, calls=%fused_computation.183 | convolution fusion | flops 2415919104 | bytes 8912896 | tf_op jit(solution)/shard_map/dot_general | solution.py:54
  222.4 3.1 add_convert_fusion.1.refs_0_
  225.6 33.3 %shard_map.249 = (bf16[1024,1024]{1,0:T(8,128)(2,1)S(1)}, f32[8,128]{1,0:T(8,128)}) custom-call(bf16[1024,1024]{1,0:T(8,128)(2,1)S(1)} %add_convert_fusion.1.refs_0_, f32[8,128]{1,0:T(8,128)S(1)} %broadcast_in_dim.115.refs_1_), custom_call_target="tpu_custom_call" | custom-call | tf_op jit(solution)/shard_map/pallas_call | solution.py:425
  259.0 2.3 fusion.16
  261.3 3.3 fusion.18
  265.5 2.9 copy-done.8
  273.3 5.4 %fusion = (f32[2,2,512]{2,1,0:T(2,128)S(1)}, f32[2,1024,512,2]{2,1,3,0:T(8,128)S(1)}) fusion(f32[2,2,512,1024]{2,3,1,0:T(8,128)} %copy-done.4, f32[2,2,512]{2,1,0:T(2,128)S(1)} %log_add_fusion, bf16[1024,2,64,1]{0,2,3,1:T(8,128)(2,1)S(1)} %bitcast.237, bf16[512,2,2,64]{0,3,2,1:T(8,128)(2,1)S(1)} %bitcast.228), kind=kOutput, calls=%fused_computation.2 | convolution fusion | flops 274724864 | bytes 17317888 | tf_op jit(solution)/shard_map/while/body/eval_jaxpr/tkgd,skd->kgts/dot_general | solution.py:114
  279.1 2.7 fusion.2
  289.6 32.5 %shard_map.250 = (bf16[1024,1024]{1,0:T(8,128)(2,1)S(1)}, f32[8,128]{1,0:T(8,128)S(1)}) custom-call(bf16[1024,1024]{1,0:T(8,128)(2,1)S(1)} %add_convert_fusion.refs_0_, f32[8,128]{1,0:T(8,128)S(1)} %select_maximum_fusion.refs_1_), custom_call_target="tpu_custom_call" | custom-call | tf_op jit(solution)/shard_map/pallas_call | solution.py:425
  322.1 2.3 fusion.17
  324.8 2.5 convolution_convert_fusion.9.refs_2_
  330.4 49.4 %shard_map.251 = (f32[16,128]{1,0:T(8,128)S(1)}, f32[128,256]{1,0:T(8,128)S(1)}, f32[128,128]{1,0:T(8,128)S(1)}, f32[128,128]{1,0:T(8,128)S(1)}, f32[128,256]{1,0:T(8,128)S(1)}) custom-call(bf16[128,128]{1,0:T(8,128)(2,1)S(1)} %bitcast.215, bf16[1024,256]{1,0:T(8,128)(2,1)S(1)} %convolution_convert_fusion.6.refs_1_, ...), custom_call_target="tpu_custom_call" | custom-call | tf_op jit(solution)/shard_map/pallas_call | solution.py:302
  380.6 5.8 %convolution_convert_fusion.2.refs_0_ = bf16[1024,1152]{1,0:T(8,128)(2,1)S(1)} fusion(bf16[1024,1024]{1,0:T(8,128)(2,1)} %multiply_convert_fusion.1, bf16[1024,1152]{1,0:T(8,128)(2,1)} %get-tuple-element.141), kind=kOutput, calls=%fused_computation.62 | convolution fusion | flops 2417098752 | bytes 6815744 | tf_op jit(solution)/shard_map/dot_general | solution.py:48
  386.5 3.2 convolution_convert_fusion.1.refs_1_
  389.7 3.2 fusion.30.refs_2_
  392.9 85.7 %shard_map.252 = (f32[128,1152]{1,0:T(8,128)S(1)}, f32[128,1152]{1,0:T(8,128)S(1)}, f32[128,1152]{1,0:T(8,128)S(1)}) custom-call(bf16[1024,1152]{1,0:T(8,128)(2,1)S(1)} %convolution_convert_fusion.2.refs_0_, bf16[1024,1152]{1,0:T(8,128)(2,1)S(1)} %convolution_convert_fusion.1.refs_1_, bf16[1024,1152]{1,0:T(8,128)(2,1)S(1)} %fusion.30.refs_2_), custom_call_target="tpu_custom_call" | custom-call | tf_op jit(solution)/shard_map/pallas_call | solution.py:302
  479.5 2.1 copy.65
  483.3 4.8 fusion.19
  488.1 2.3 add_convert_fusion.2
  (253 shorter events, 47.7 us)
Async XLA Ops:
  7.2 480.9 %reduce-scatter.2.cloned.1.call-start = ((), (), s32[]{:S(2)}) async-start(), calls=%async_computation.1 | async-start | bytes 2621440 | tf_op jit(solution)/shard_map/reduce_scatter | solution.py:542
  39.7 6.0 %copy-start.31 = (bf16[1024,128]{1,0:T(8,128)(2,1)S(1)}, bf16[1024,128]{1,0:T(8,128)(2,1)}, u32[]{:S(2)}) copy-start(bf16[1024,128]{1,0:T(8,128)(2,1)} %get-tuple-element.85) | copy-start | bytes 786436
  40.5 6.7 %copy-start.49 = (f32[8,1,128]{2,1,0:T(1,128)}, f32[8,1,128]{2,1,0:T(1,128)S(1)}, u32[]{:S(2)}) copy-start(f32[8,1,128]{2,1,0:T(1,128)S(1)} %get-tuple-element.159) | copy-start | bytes 12292
  40.5 58.4 %copy-start.53 = (f32[8,1,128]{2,1,0:T(1,128)}, f32[8,1,128]{2,1,0:T(1,128)S(1)}, u32[]{:S(2)}) copy-start(f32[8,1,128]{2,1,0:T(1,128)S(1)} %get-tuple-element.160) | copy-start | bytes 12292
  43.4 3.8 copy-start.55
  43.5 7.8 %copy-start.66 = (f32[64]{0:T(128)}, f32[64]{0:T(128)S(1)}, u32[]{:S(2)}) copy-start(f32[64]{0:T(128)S(1)} %reshape.273) | copy-start | bytes 772
  45.7 5.0 %copy-start.5 = (bf16[1024,1024]{1,0:T(8,128)(2,1)}, bf16[1024,1024]{1,0:T(8,128)(2,1)S(1)}, u32[]{:S(2)}) copy-start(bf16[1024,1024]{1,0:T(8,128)(2,1)S(1)} %fusion.14) | copy-start | bytes 6291460
  45.7 4.0 copy-start.68
  45.7 4.1 copy-start.35
  52.0 7.5 %copy-start.27 = (bf16[1024,2,32]{0,2,1:T(8,128)(2,1)}, bf16[1024,2,32]{0,2,1:T(8,128)(2,1)S(1)}, u32[]{:S(2)}) copy-start(bf16[1024,2,32]{0,2,1:T(8,128)(2,1)S(1)} %get-tuple-element.152) | copy-start | bytes 393220
  52.0 9.0 %copy-start.38 = (bf16[512,128]{0,1:T(8,128)(2,1)}, bf16[512,128]{0,1:T(8,128)(2,1)S(1)}, u32[]{:S(2)}) copy-start(bf16[512,128]{0,1:T(8,128)(2,1)S(1)} %slice.158) | copy-start | bytes 393220
  52.1 7.4 %copy-start.15 = (bf16[512,4,64]{0,2,1:T(8,128)(2,1)}, bf16[512,4,64]{0,2,1:T(8,128)(2,1)S(1)}, u32[]{:S(2)}) copy-start(bf16[512,4,64]{0,2,1:T(8,128)(2,1)S(1)} %get-tuple-element.155) | copy-start | bytes 786436
  62.4 33.3 %copy-start.1 = (bf16[1024,1024]{1,0:T(8,128)(2,1)S(1)}, bf16[1024,1024]{1,0:T(8,128)(2,1)}, u32[]{:S(2)}) copy-start(bf16[1024,1024]{1,0:T(8,128)(2,1)} %param.15) | copy-start | bytes 6291460
  97.1 103.7 %copy-start.51 = (f32[1024]{0:T(1024)}, f32[1024]{0:T(1024)S(1)}, u32[]{:S(2)}) copy-start(f32[1024]{0:T(1024)S(1)} %fusion.75) | copy-start | bytes 12292
  195.4 5.4 %copy-start.21 = (bf16[1024,1024]{1,0:T(8,128)(2,1)S(1)}, bf16[1024,1024]{1,0:T(8,128)(2,1)}, u32[]{:S(2)}) copy-start(bf16[1024,1024]{1,0:T(8,128)(2,1)} %multiply_convert_fusion.1) | copy-start | bytes 6291460
  195.4 5.4 %copy-start.69 = (bf16[1024,1152]{1,0:T(8,128)(2,1)S(1)}, bf16[1024,1152]{1,0:T(8,128)(2,1)}, u32[]{:S(2)}) copy-start(bf16[1024,1152]{1,0:T(8,128)(2,1)} %get-tuple-element.91) | copy-start | bytes 7077892
  216.9 5.4 %copy-start.70 = (bf16[1024,1152]{1,0:T(8,128)(2,1)S(1)}, bf16[1024,1152]{1,0:T(8,128)(2,1)}, u32[]{:S(2)}) copy-start(bf16[1024,1152]{1,0:T(8,128)(2,1)} %get-tuple-element.91) | copy-start | bytes 7077892
  217.0 5.4 %copy-start.72 = (bf16[1024,1152]{1,0:T(8,128)(2,1)S(1)}, bf16[1024,1152]{1,0:T(8,128)(2,1)}, u32[]{:S(2)}) copy-start(bf16[1024,1152]{1,0:T(8,128)(2,1)} %get-tuple-element.140) | copy-start | bytes 7077892
  222.4 36.5 %copy-start.2 = (bf16[1024,1024]{1,0:T(8,128)(2,1)S(1)}, bf16[1024,1024]{1,0:T(8,128)(2,1)}, u32[]{:S(2)}) copy-start(bf16[1024,1024]{1,0:T(8,128)(2,1)} %param.15) | copy-start | bytes 6291460
  222.4 36.5 %copy-start.52 = (f32[1024]{0:T(1024)S(1)}, f32[1024]{0:T(1024)}, u32[]{:S(2)}) copy-start(f32[1024]{0:T(1024)} %copy-done.51) | copy-start | bytes 12292
  222.4 36.5 %copy-start.54 = (f32[8,1,128]{2,1,0:T(1,128)S(1)}, f32[8,1,128]{2,1,0:T(1,128)}, u32[]{:S(2)}) copy-start(f32[8,1,128]{2,1,0:T(1,128)} %copy-done.53) | copy-start | bytes 12292
  225.6 35.7 %copy-start.57 = (f32[1024]{0:T(1024)S(1)}, f32[1024]{0:T(1024)}, u32[]{:S(2)}) copy-start(f32[1024]{0:T(1024)} %copy-done.56) | copy-start | bytes 12292
  225.6 35.7 %copy-start.18 = (bf16[1024,1024]{1,0:T(8,128)(2,1)S(1)}, bf16[1024,1024]{1,0:T(8,128)(2,1)}, u32[]{:S(2)}) copy-start(bf16[1024,1024]{1,0:T(8,128)(2,1)} %param.16) | copy-start | bytes 6291460
  264.6 4.7 copy-start.9
  264.6 3.7 copy-start.8
  273.3 5.4 %slice-start = ((s8[8388608]{0:T(1024)(128)(4,1)}), s8[4194304]{0:T(1024)(128)(4,1)S(1)}, s32[]{:S(2)}) async-start(s8[8388608]{0:T(1024)(128)(4,1)} %bitcast.217), calls=%async_computation.2 | async-start | bytes 8388608
  273.3 5.8 %slice-start.1 = ((s8[8388608]{0:T(1024)(128)(4,1)}), s8[4194304]{0:T(1024)(128)(4,1)S(1)}, s32[]{:S(2)}) async-start(s8[8388608]{0:T(1024)(128)(4,1)} %bitcast.217), calls=%async_computation.3 | async-start | bytes 8388608
  288.7 33.4 %copy-start.3 = (bf16[1024,1024]{1,0:T(8,128)(2,1)S(1)}, bf16[1024,1024]{1,0:T(8,128)(2,1)}, u32[]{:S(2)}) copy-start(bf16[1024,1024]{1,0:T(8,128)(2,1)} %param.15) | copy-start | bytes 6291460
  288.7 33.4 %copy-start.50 = (f32[8,1,128]{2,1,0:T(1,128)S(1)}, f32[8,1,128]{2,1,0:T(1,128)}, u32[]{:S(2)}) copy-start(f32[8,1,128]{2,1,0:T(1,128)} %copy-done.49) | copy-start | bytes 12292
  289.6 34.9 %copy-start.63 = (bf16[1024]{0:T(1024)(128)(2,1)S(1)}, bf16[1024]{0:T(1024)(128)(2,1)}, u32[]{:S(2)}) copy-start(bf16[1024]{0:T(1024)(128)(2,1)} %get-tuple-element.130) | copy-start | bytes 6148
  380.6 5.8 %copy-start.22 = (bf16[1024,1024]{1,0:T(8,128)(2,1)S(1)}, bf16[1024,1024]{1,0:T(8,128)(2,1)}, u32[]{:S(2)}) copy-start(bf16[1024,1024]{1,0:T(8,128)(2,1)} %multiply_convert_fusion.1) | copy-start | bytes 6291460
  380.6 5.9 %copy-start.73 = (bf16[1024,1152]{1,0:T(8,128)(2,1)S(1)}, bf16[1024,1152]{1,0:T(8,128)(2,1)}, u32[]{:S(2)}) copy-start(bf16[1024,1152]{1,0:T(8,128)(2,1)} %get-tuple-element.140) | copy-start | bytes 7077892
  (48 other events, 94.2 us)
Sparse Core Ops, SparseCore 0:
  215.6 50.9 reduce-scatter.1
